TPU v7x, 128 devices: a whole 4x4x4 slice. The times are simulated.
128 devices in a mesh: ctx: 32 (over y, z, core), wsh: 4 (over x).
Axes of the slice: x: 4, y: 4, z: 4, core: 2. Of those that a mesh axis runs over, the one named last changes fastest.
Arguments:
- tokens: bfloat16 [24576, 512], P(('wsh', 'ctx')), may hold values from -6 to 6
- cotangent: bfloat16 [24576, 512], P(('wsh', 'ctx')), may hold values from -6 to 6
- ln_gain: float32 [512], replicated, may hold values from 0.5 to 1.5
- ln_bias: float32 [512], replicated, may hold values from -1.75 to 1.75
- biases: float32 [4608], replicated, may hold values from -1.75 to 1.75
- w_qkv: float32 [512, 1536], P('wsh'), may hold values from -0.25 to 0.25
- w_out: float32 [512, 512], P('wsh'), may hold values from -1.5 to 1.5
- w_in: float32 [512, 2048], P('wsh'), may hold values from -0.25 to 0.25
- w_fin: float32 [2048, 512], P('wsh'), may hold values from -0.125 to 0.125
- mom_qkv: float32 [512, 1536], P('wsh'), may hold values from -1792 to 1792
- mom_out: float32 [512, 512], P('wsh'), may hold values from -48 to 48
- mom_in: float32 [512, 2048], P('wsh'), may hold values from -224 to 224
- mom_fin: float32 [2048, 512], P('wsh'), may hold values from -384 to 384
- vec_mom: float32 [5632], replicated, may hold values from -1792 to 1792
- starts: int32 [4], replicated, may hold values from 1 to 18623, as said below
Outputs:
- block_out: bfloat16 [24576, 512], P(('wsh', 'ctx'))
- grad_tokens: float32 [24576, 512], P(('wsh', 'ctx'))
- new_mom_qkv: float32 [512, 1536], P('wsh')
- new_w_qkv: float32 [512, 1536], P('wsh')
- new_mom_out: float32 [512, 512], P('wsh')
- new_w_out: float32 [512, 512], P('wsh')
- new_mom_in: float32 [512, 2048], P('wsh')
- new_w_in: float32 [512, 2048], P('wsh')
- new_mom_fin: float32 [2048, 512], P('wsh')
- new_w_fin: float32 [2048, 512], P('wsh')
- new_vec_mom: float32 [5632], replicated
- new_vectors: float32 [5632], replicated
Inputs may be any that keep to these rules, and one draw needn't show every extreme that they name: Packed row g holds tokens g * 6144 to (g + 1) * 6144 - 1; a sequence starts at its first token and another at starts[g], which lies among the row's first 192 tokens and is not its first token.
All inputs are finite; a program needn't handle non-finite values.
Results may differ from a plain program's by a relative error of at most 0.007.
The roundings to bfloat16 on the way count: a program that leaves them out, or rounds other values in their place, can miss the bound.
Values may be sent and summed in bfloat16 or wider, within the bound.
A program may use at most 320 MiB of HBM per device.

v0:
```python
import functools
import math
import types

import jax
import jax.numpy as jnp
from jax import lax
from jax.experimental import pallas as pl
from jax.experimental.pallas import tpu as pltpu
from jax.sharding import PartitionSpec as P

f32 = jnp.float32
bf16 = jnp.bfloat16
MESH = pl.DeviceIdType.MESH
HEADS = 8
HD = 64
ROT = 16
D = 512
TOK = 192
GROUP = 6144
QB = 256
NQB = 6
HB = 128
UU = 8
TT = 4
NS_ITERS = 5
C1, C2, C3 = 3.4445, -4.775, 2.0315
MU, LR, WD = 0.95, 0.6, 0.01
VMU, VLR = 0.9, 0.0005
R_QKV, R_OUT, R_IN, R_FIN = 48, 16, 64, 64

VM = pl.BlockSpec(memory_space=pltpu.VMEM)
SM = pl.BlockSpec(memory_space=pltpu.SMEM)
ANY = pl.BlockSpec(memory_space=pl.ANY)
DMA = pltpu.SemaphoreType.DMA


def dot(a, b):
    return jnp.dot(a, b, preferred_element_type=f32)


def dot_nt(a, b):
    return lax.dot_general(a, b, (((1,), (1,)), ((), ())), preferred_element_type=f32)


def dot_tn(a, b):
    return lax.dot_general(a, b, (((0,), (0,)), ((), ())), preferred_element_type=f32)


def coords():
    c = lax.axis_index("ctx")
    return c // 8, (c // 2) % 4, c % 2, lax.axis_index("wsh")


def at(y, z, s, x):
    return {"ctx": (y * 4 + z) * 2 + s, "wsh": x}


def tell(partners):
    sem = pltpu.get_barrier_semaphore()
    for p in partners:
        pl.semaphore_signal(sem, inc=1, device_id=p, device_id_type=MESH)


def tell_slab():
    c = lax.axis_index("ctx")
    sem = pltpu.get_barrier_semaphore()

    def one(d, _):
        pl.semaphore_signal(
            sem, inc=1, device_id={"ctx": lax.rem(c + d, 32)}, device_id_type=MESH
        )
        return 0

    lax.fori_loop(1, 32, one, 0)


def met(count):
    pl.semaphore_wait(pltpu.get_barrier_semaphore(), count)


def wait_for(ref, sem):
    pltpu.make_async_copy(ref, ref, sem).wait()


def loop(lo, hi, f):
    def step(i, _):
        f(i)
        return 0

    lax.fori_loop(lo, hi, step, 0)


AXES = ("y", "z", "x")


def moved(axis, d):
    y, z, s, x = coords()
    if axis == "y":
        return at((y + d) % 4, z, s, x)
    if axis == "z":
        return at(y, (z + d) % 4, s, x)
    return at(y, z, s, (x + d) % 4)


def other_core():
    y, z, s, x = coords()
    return at(y, z, 1 - s, x)


def lines(axes=AXES):
    return [moved(a, d) for a in axes for d in (1, 2, 3)]


def send(src, dst, ss, rs, dev):
    cp = pltpu.make_async_remote_copy(
        src_ref=src, dst_ref=dst, send_sem=ss, recv_sem=rs, device_id=dev, device_id_type=MESH
    )
    cp.start()
    return cp


ALL = slice(None)


class Gather:
    def __init__(self, items, ss, rs):
        self.items, self.ss, self.rs = items, ss, rs

    def begin(self):
        y, z, s, x = coords()
        for i, (get, y_first) in enumerate(self.items):
            piece = get(y, z, s)
            for d in (1, 2, 3):
                send(
                    piece, piece, self.ss.at[i, 0], self.rs.at[i, 0], moved("y" if y_first else "z", d)
                )

    def turn(self):
        y, z, s, x = coords()
        three = pl.ds(0, 3)
        for i, (get, y_first) in enumerate(self.items):
            pieces = get(three, z, s) if y_first else get(y, three, s)
            wait_for(pieces, self.ss.at[i, 0])
            wait_for(pieces, self.rs.at[i, 0])
        self.second = {}
        for i, (get, y_first) in enumerate(self.items):
            piece = get(ALL, z, s) if y_first else get(y, ALL, s)
            for d in (1, 2, 3):
                to = moved("z" if y_first else "y", d)
                self.second[i, d] = send(piece, piece, self.ss.at[i, 1], self.rs.at[i, d], to)
        for i, (get, y_first) in enumerate(self.items):
            piece = get(ALL, z, s) if y_first else get(y, ALL, s)
            send(piece, piece, self.ss.at[i, 2], self.rs.at[i, 4], other_core())

    def pass_on(self):
        y, z, s, x = coords()
        for d in (1, 3, 2):
            for i, (get, y_first) in enumerate(self.items):
                self.second[i, d].wait_recv()
                piece = get(ALL, (z - d) % 4, s) if y_first else get((y - d) % 4, ALL, s)
                send(piece, piece, self.ss.at[i, 2], self.rs.at[i, 4], other_core())

    def end(self):
        three = pl.ds(0, 3)
        for i, (get, y_first) in enumerate(self.items):
            wait_for(get(ALL, three, 0) if y_first else get(three, ALL, 0), self.ss.at[i, 1])
            wait_for(get(ALL, ALL, 0), self.ss.at[i, 2])
            wait_for(get(ALL, ALL, 0), self.rs.at[i, 4])


def split(v):
    hi = v.astype(bf16)
    return hi, (v - hi.astype(f32)).astype(bf16)


class Reduce:
    def __init__(self, src, parts, bufs, ss, rs):
        self.src, self.parts, self.ss, self.rs = src, parts, ss, rs
        y, z, s, x = coords()
        self.me = {"y": y, "z": z, "x": x}
        self.bufs = [bufs[5 * i : 5 * i + 5] for i in range(len(parts))]

    @staticmethod
    def scratch(parts):
        out = []
        for lo, n, order, paired in parts:
            out += [
                pltpu.VMEM((3, 4, 4, n, 128), bf16),
                pltpu.VMEM((4, 4, n, 128), bf16),
                pltpu.VMEM((3, 4, n, 128), bf16),
                pltpu.VMEM((4, n, 128), bf16),
                pltpu.VMEM((3, n, 128), bf16),
            ]
        return out

    @staticmethod
    def summed(pieces, paired):
        v = functools.reduce(lambda a, b: a + b, [p.astype(f32) for p in pieces])
        if not paired:
            return v.astype(bf16)
        half = v.shape[-2] // 2
        return jnp.concatenate(split(v[..., :half, :] + v[..., half:, :]), axis=-2)

    def begin(self, stage):
        for d in (2, 1, 3):
            for i, (lo, n, order, paired) in enumerate(self.parts):
                r1, h1, r2, h2, r3 = self.bufs[i]
                axis = order[stage]
                place = (self.me[axis] + d) % 4
                left = [a for a in AXES if a not in order[:stage]]
                index = tuple(place if a == axis else ALL for a in left)
                if stage == 0:
                    src = self.src.at[index + (pl.ds(lo, n),)]
                else:
                    src = (h1, h2)[stage - 1].at[index]
                send(
                    src, (r1, r2, r3)[stage].at[d - 1],
                    self.ss.at[stage, i], self.rs.at[stage, i], moved(axis, d),
                )

    def end(self, stage):
        out = []
        for i, (lo, n, order, paired) in enumerate(self.parts):
            r1, h1, r2, h2, r3 = self.bufs[i]
            wait_for((r1, r2, r3)[stage], self.ss.at[stage, i])
            wait_for((r1, r2, r3)[stage], self.rs.at[stage, i])
            mine = self.me[order[stage]]
            if stage == 0:
                axis = AXES.index(order[0])

                def add(a, _, axis=axis, mine=mine, lo=lo, n=n, paired=paired, r1=r1, h1=h1):
                    index = [a, ALL]
                    index.insert(axis, mine)
                    own = self.src[tuple(index) + (slice(lo, lo + n),)]
                    h1[a] = self.summed([own, r1[0, a], r1[1, a], r1[2, a]], paired)
                    return 0

                lax.fori_loop(0, 4, add, 0)
            elif stage == 1:
                left = [a for a in AXES if a != order[0]]
                first = left.index(order[1]) == 0
                own = h1[mine] if first else h1[:, mine]
                h2[...] = self.summed([own, r2[0], r2[1], r2[2]], paired)
            else:
                v = h2[mine].astype(f32) + r3[0].astype(f32) + r3[1].astype(f32) + r3[2].astype(f32)
                if paired:
                    v = v[: n // 2] + v[n // 2 :]
                out.append(v)
        return out


MLP_PARTS = ((0, 48, ("y", "z", "x"), False), (48, 48, ("z", "x", "y"), False), (96, 32, ("x", "y", "z"), False))
ATT_PARTS = ((0, 32, ("y", "z", "x"), False), (32, 16, ("z", "x", "y"), False), (48, 32, ("x", "y", "z"), True))


def norm_parts(x_ref, gain, shift):
    xf = x_ref[...].astype(f32)
    centered = xf - jnp.mean(xf, axis=1, keepdims=True)
    inv = lax.rsqrt(jnp.mean(centered * centered, axis=1, keepdims=True) + 1e-05)
    normed = centered * inv
    hidden = (normed * gain + shift).astype(bf16)
    return xf, inv, normed, hidden


def turn(v, co, s1, s2):
    return v * co + pltpu.roll(v, 120, 1) * s1 + pltpu.roll(v, 8, 1) * s2


def rolled(ref, x):
    parts = [ref[:, pl.ds(pl.multiple_of((x + d) % 4 * 128, 128), 128)] for d in range(4)]
    return jnp.concatenate(parts, axis=1)


def unroll(v, ref, x):
    for d in range(4):
        ref[:, pl.ds(pl.multiple_of((x + d) % 4 * 128, 128), 128)] = v[:, 128 * d : 128 * d + 128]
    return ref[...]


def rotary(starts_ref, x, c):
    bnd = starts_ref[x] - x * GROUP
    place = c * TOK + lax.broadcasted_iota(jnp.int32, (TOK, 128), 0)
    pos = (place - jnp.where(place >= bnd, bnd, 0)).astype(f32)
    lane = lax.broadcasted_iota(jnp.int32, (TOK, 128), 1) % HD
    freq = jnp.zeros((TOK, 128), f32)
    for i in range(ROT // 2):
        freq = jnp.where(lane % 8 == i, 10000.0 ** (-2.0 * i / ROT), freq)
    angle = pos * jnp.where(lane < ROT, freq, 0.0)
    co, si = jnp.cos(angle), jnp.sin(angle)
    return co, jnp.where(lane < 8, -si, 0.0), jnp.where(lane < 8, 0.0, si)


def wide(w, first, count):
    blocks = [w[(first + i) // 4, (first + i) % 4].reshape(512, 128) for i in range(count)]
    return jnp.concatenate(blocks, axis=1) if count > 1 else blocks[0]


def query_home(piece):
    block = piece // 4
    part = block % 8
    low = part < 4
    return jnp.where(low, part, 7 - part), 2 * (block // 8) + jnp.where(low, 0, 1), piece % 4


def query_block(t, j):
    if isinstance(t, int):
        return 8 * (t // 2) + (j if t % 2 == 0 else 7 - j)
    return 8 * (t // 2) + jnp.where(t % 2 == 0, j, 7 - j)


def front_phase(r):
    y, z, s, x = coords()
    c = lax.axis_index("ctx")
    p = c // 2
    w1, w2, w3, kvs, qds, kv, qd = r.w1, r.w2, r.w3, r.kvs, r.qds, r.kv, r.qd
    ks, kr, qs, qr, cs, cr = r.ks, r.kvr, r.qs, r.qr, r.cs, r.cr
    bias_ref = r.bias
    tell_slab()
    tell(lines(("x",)))
    loads = [
        pltpu.make_async_copy(src, dst, r.lsem.at[k])
        for k, (src, dst) in enumerate(
            ((r.wq, r.fq), (r.wo, r.fo), (r.wi, r.fi), (r.wf, r.ff), (r.x_in, r.x), (r.dy_in, r.dy))
        )
    ]
    for cp in loads:
        cp.start()
    momenta_begin(r)
    for cp in loads:
        cp.wait()
    for b in range(16):
        w = r.fq[:, 128 * b : 128 * b + 128] if b < 12 else r.fo[:, 128 * b - 1536 : 128 * b - 1408]
        w1[b // 4, b % 4, 0] = w.astype(bf16).reshape(2, 64, 128)
        w2[b // 4, b % 4, 0] = r.fi[:, 128 * b : 128 * b + 128].astype(bf16).reshape(2, 64, 128)
    w3[0] = r.ff[...].astype(bf16).reshape(4, 4, 2, 16, 512)
    met(34)
    slab, direct = pl.ds(0, 32), pl.ds(32, 32)

    def along_x(k, piece):
        return [
            send(piece(0), piece(4 - d), r.xs.at[k, d - 1], r.xr.at[k, d - 1], moved("x", d))
            for d in (1, 2, 3)
        ]

    low, high = pl.ds(0, 256), pl.ds(256, 256)
    own_cps = along_x(0, lambda d: w1.at[y, z, d, s, slab])
    late_cps = along_x(4, lambda d: w3.at[d, y, z, s, :, high])
    direct_cps = along_x(1, lambda d: w1.at[:, :, d, s, direct])
    co, s1, s2 = rotary(r.starts, x, c)
    r.co[...], r.s1[...], r.s2[...] = co, s1, s2
    xf, inv, normed, hidden = norm_parts(r.x, r.gain[...], r.shift[...])
    r.hid[...] = hidden
    hidden_r = rolled(r.hid, x)
    dy = r.dy[...]
    for cp in own_cps:
        cp.wait()
    others = pl.ds(1, 3)
    early = Gather(
        [
            (lambda a, b, e: w1.at[a, b, others, e, pl.ds(0, 16)], True),
            (lambda a, b, e: w1.at[a, b, others, e, pl.ds(16, 16)], False),
        ],
        r.sa, r.ra,
    )
    late = Gather(
        [
            (lambda a, b, e: w3.at[others, a, b, e, :, pl.ds(256, 128)], True),
            (lambda a, b, e: w3.at[others, a, b, e, :, pl.ds(384, 128)], False),
        ],
        r.sb, r.rb,
    )

    def to_core(k, cps, piece):
        out = []
        for d in (1, 3, 2):
            cps[d - 1].wait_recv()
            got = piece(4 - d)
            out.append(send(got, got, r.ys.at[k, d - 1], r.yr.at[k, d - 1], other_core()))
        for cp in cps:
            cp.wait_send()
        return out

    early.begin()
    early.turn()
    passed = to_core(0, direct_cps, lambda d: w1.at[:, :, d, s, direct])
    in_cps = along_x(2, lambda d: w2.at[:, :, d, s])
    fin_cps = along_x(3, lambda d: w3.at[d, :, :, s, :, low])
    early.pass_on()
    for cp in late_cps:
        cp.wait()
    late.begin()
    early.end()
    for cp in passed:
        cp.wait()
    left = lax.broadcasted_iota(jnp.int32, (TOK, 128), 1) < 64
    dctx = unroll(dot_nt(dy, wide(w1, 12, 4)), r.wide_f, x)
    for half in range(2):
        thirds = []
        for third in range(3):
            b = third * 4 + 2 * half
            thirds.append(dot(hidden_r, wide(w1, b, 2)) + bias_ref[b * 128 : b * 128 + 256][None, :])
        for e in range(2):
            lanes = slice(128 * e, 128 * e + 128)
            q = turn(thirds[0][:, lanes], co, s1, s2).astype(bf16).astype(f32) * 0.125
            k = turn(thirds[1][:, lanes], co, s1, s2)
            v = thirds[2][:, lanes]
            pair = 2 * half + e
            g = dctx[:, pair * 128 : pair * 128 + 128]
            h = 2 * pair
            kvs[h] = jnp.where(left, k, pltpu.roll(v, 64, 1)).astype(bf16)
            kvs[h + 1] = jnp.where(left, pltpu.roll(k, 64, 1), v).astype(bf16)
            qds[h] = jnp.where(left, q, pltpu.roll(g, 64, 1)).astype(bf16)
            qds[h + 1] = jnp.where(left, pltpu.roll(q, 64, 1), g).astype(bf16)

    def kv_copy(d):
        to = lax.rem(p + d, 16)
        return pltpu.make_async_remote_copy(
            src_ref=kvs.at[to // 2], dst_ref=kv.at[pl.ds(c * TOK, TOK)], send_sem=ks, recv_sem=kr,
            device_id={"ctx": to * 2 + s}, device_id_type=MESH,
        )

    def across(d):
        block = kv.at[pl.ds((lax.rem(p + 16 - d, 16) * 2 + s) * TOK, TOK)]
        return pltpu.make_async_remote_copy(
            src_ref=block, dst_ref=block, send_sem=cs, recv_sem=cr,
            device_id={"ctx": p * 2 + 1 - s}, device_id_type=MESH,
        )

    def each_query(k):
        h, i = k // 3, k % 3
        j, t, quarter = query_home(3 * c + i)
        to = 4 * h + j
        src = qds.at[h, pl.ds(64 * i, 64)]
        dst = qd.at[t, pl.ds(64 * quarter, 64)]

        @pl.when(to == c)
        def _():
            pltpu.make_async_copy(src, dst, qr).start()
            pltpu.make_async_copy(src, r.spare.at[i], qs).start()

        @pl.when(to != c)
        def _():
            pltpu.make_async_remote_copy(
                src_ref=src, dst_ref=dst, send_sem=qs, recv_sem=qr,
                device_id={"ctx": to}, device_id_type=MESH,
            ).start()

    own = pltpu.make_async_copy(kvs.at[p // 2], kv.at[pl.ds(c * TOK, TOK)], r.own_sem)
    own.start()
    late.turn()
    loop(1, 16, lambda d: kv_copy(d).start())
    loop(0, 24, each_query)
    own.wait()

    r.acc[...] = jnp.zeros_like(r.acc)
    late.pass_on()
    late.end()
    passed = to_core(1, in_cps, lambda d: w2.at[:, :, d, s])
    passed += to_core(2, fin_cps, lambda d: w3.at[d, :, :, s, :, low])
    for cp in passed:
        cp.wait()
    root = math.sqrt(2.0 / math.pi)
    mlp = jnp.zeros((TOK, D), f32)
    dh = jnp.zeros((TOK, D), f32)
    for i in range(4):
        if i == 2:
            wait_for(kv.at[pl.ds(0, 15 * TOK)], kr)
            loop(0, 16, lambda d: across(d).start())
        w_in = wide(w2, 4 * i, 4)
        w_fin = w3[(i + 4 - x) % 4].reshape(512, 512)
        pre = dot(hidden_r, w_in) + bias_ref[2048 + 512 * i : 2560 + 512 * i][None, :]
        sq = pre * pre
        th = jnp.tanh(root * (pre + 0.044715 * (pre * sq)))
        act = (0.5 * pre * (1.0 + th)).astype(bf16)
        slope = 0.5 * (1.0 + th) + (0.5 * root) * pre * (1.0 - th * th) * (
            1.0 + (3.0 * 0.044715) * sq
        )
        dpre = (dot_nt(dy, w_fin) * slope).astype(bf16)
        mlp = mlp + dot(act, w_fin)
        dh = dh + dot_nt(dpre, w_in)
        r.v0[6 + i : 7 + i, :] = jnp.sum(dpre.astype(f32), axis=0, keepdims=True)
        g_in = dot_tn(dpre, hidden).astype(bf16).reshape(4, 2, 64, 512)
        g_fin = dot_tn(act, dy).astype(bf16).reshape(4, 4, 2, 16, 512)
        for b in range(4):
            lanes = slice(128 * b, 128 * b + 128)
            r.gm[i, :, :, b, 0:64] = g_in[..., lanes]
            r.gm[:, :, :, i, 64 + 16 * b : 80 + 16 * b] = g_fin[..., lanes]
    r.res[...] = xf + mlp + (bias_ref[4096:4608] + bias_ref[1536:2048])[None, :]
    r.dh[...] = dh
    chip = send(r.gm.at[:, :, 1 - s], r.rcm, r.m_s.at[0], r.m_r.at[0], other_core())
    wait_for(kv.at[pl.ds(0, 15 * TOK)], ks)
    wait_for(qd, qs)
    wait_for(qd, qr)
    wait_for(kv.at[pl.ds(0, 16 * TOK)], cs)
    wait_for(kv.at[pl.ds(0, 16 * TOK)], cr)
    return chip


RETURNS = ((14, 16), (11, 14), (8, 11), (6, 8), (3, 6), (0, 3))


def attention_phase(r, chip):
    kvt, acc, s_sc, p_sc, m_sc, cqs = r.kvt, r.acc, r.s_sc, r.p_sc, r.m_sc, r.cqs
    half, other, both, rcm, hbuf = r.half, r.other, r.both, r.rcm, r.hbuf
    cq, kr, kv_ref, qd_ref, gm_ref = r.cq, r.kr, r.kv, r.qd, r.gm
    ws, wr, ss, sr, qs, qr = r.ws, r.wr, r.bs, r.br, r.rqs, r.rqr
    y, z, s, x = coords()
    c = lax.axis_index("ctx")
    p = c // 2
    h = c // 4
    j = c % 4
    n = kv_ref.shape[0]
    bnd = r.starts[x] - x * GROUP

    def prepare(i, _):
        o = pl.multiple_of(i * QB, QB)
        kvt[:, pl.ds(o, QB)] = kv_ref[pl.ds(o, QB), :].T
        return 0

    lax.fori_loop(0, n // QB, prepare, 0)
    lane = lax.broadcasted_iota(jnp.int32, (QB, 128), 1)

    def block(t):
        qb = query_block(t, j)
        qd = qd_ref[t]
        w1 = jnp.where(lane < 64, qd, jnp.zeros_like(qd))
        w2 = jnp.where(lane < 64, jnp.zeros_like(qd), qd)
        q_t = w1.T
        d_t = w2.T

        def scores(kt, masked, carry, tiles, first=False):
            m8, l8, r8 = carry
            for u in range(2 * tiles):
                o = pl.multiple_of(kt * QB + u * HB, HB)
                rows = kv_ref[pl.ds(o, HB), :]
                s = dot(rows, q_t)
                if masked and not (first and u > 1):
                    kp = o + lax.broadcasted_iota(jnp.int32, (HB, QB), 0)
                    qp = qb * QB + lax.broadcasted_iota(jnp.int32, (HB, QB), 1)
                    s = jnp.where((kp <= qp) & ((kp >= bnd) == (qp >= bnd)), s, -1e30)
                s = s.reshape(HB // 8, 8, QB)
                dp = dot(rows, d_t)
                p_sc[pl.ds(o, HB), :] = dp
                mn = jnp.maximum(m8, jnp.max(s, axis=0))
                e = jnp.exp(s - mn[None])
                s_sc[pl.ds(o, HB), :] = e.reshape(HB, QB)
                m_sc[2 * kt + u] = mn
                al = jnp.exp(m8 - mn)
                l8 = l8 * al + jnp.sum(e, axis=0)
                r8 = r8 * al + jnp.sum(e * dp.reshape(HB // 8, 8, QB), axis=0)
                m8 = mn
            return m8, l8, r8

        zero = jnp.zeros((8, QB), f32)
        base = t // 2 * 8
        tail = (qb - base) // TT + 1
        carry = lax.fori_loop(
            0, tail, lambda g, c: scores(base + TT * g, True, c, TT),
            (jnp.full((8, QB), -1e30, f32), zero, zero),
        )
        if base > 0:
            carry = scores(0, True, carry, UU, True)
        carry = lax.fori_loop(
            1, base // UU, lambda g, c: scores(g * UU, False, c, UU), carry
        )
        m8, l8, r8 = carry
        m = jnp.max(m8, axis=0, keepdims=True)
        w = jnp.exp(m8 - m)
        l = jnp.sum(l8 * w, axis=0, keepdims=True)
        lse = m + jnp.log(l)
        rd = jnp.sum(r8 * w, axis=0, keepdims=True) / l

        def grads(kt, carry, tiles):
            c_t, g_t = carry
            for u in range(tiles):
                o = pl.multiple_of((kt + u) * QB, QB)
                e = s_sc[pl.ds(o, QB), :].reshape(2, HB // 8, 8, QB)
                w0 = jnp.exp(m_sc[2 * (kt + u)] - lse)
                w1_ = jnp.exp(m_sc[2 * (kt + u) + 1] - lse)
                p = jnp.concatenate([e[0] * w0[None], e[1] * w1_[None]], axis=0).reshape(QB, QB)
                pb = p.astype(bf16)
                ds = (p * (p_sc[pl.ds(o, QB), :] - rd)).astype(bf16)
                c_t = c_t + dot(kvt[64:128, pl.ds(o, QB)], pb)
                g_t = g_t + dot(kvt[0:64, pl.ds(o, QB)], ds)
                acc[pl.ds(o, QB), :] += dot(ds, w1) + dot(pb, w2)
            return c_t, g_t

        z = jnp.zeros((64, QB), f32)
        c = lax.fori_loop(0, base // UU, lambda g, c: grads(g * UU, c, UU), (z, z))
        c_t, g_t = lax.fori_loop(0, tail, lambda g, c: grads(base + TT * g, c, TT), c)
        cqs[t] = jnp.concatenate([g_t * 0.125, c_t], axis=0).T.astype(bf16)

    def each_query(t, quarter):
        piece = 4 * query_block(t, j) + quarter
        to, i = piece // 3, piece % 3
        src = cqs.at[t, pl.ds(64 * quarter, 64)]
        dst = cq.at[h, pl.ds(64 * i, 64)]

        @pl.when(to == c)
        def _():
            pltpu.make_async_copy(src, dst, qr).start()
            pltpu.make_async_copy(src, r.spare.at[3 + i], qs).start()

        @pl.when(to != c)
        def _():
            pltpu.make_async_remote_copy(
                src_ref=src, dst_ref=dst, send_sem=qs, recv_sem=qr,
                device_id={"ctx": to}, device_id_type=MESH,
            ).start()

    def return_queries(t):
        loop(0, 4, lambda quarter: each_query(t, quarter))

    swaps = {}

    def exchange(g):
        lo, hi = RETURNS[g]

        def low(i):
            o = pl.multiple_of((2 * i + 1 - s) * TOK, TOK)
            half[i] = acc[pl.ds(o, TOK), :].astype(bf16)

        loop(lo, hi, low)
        part = pl.ds(lo, hi - lo)
        swaps[g] = send(half.at[part], other.at[part], ws.at[g], wr.at[g], other_core())

    def block_copy(i):
        return pltpu.make_async_remote_copy(
            src_ref=both.at[i], dst_ref=kr.at[h, p % 2], send_sem=ss, recv_sem=sr,
            device_id={"ctx": i * 2 + s}, device_id_type=MESH,
        )

    def push(g):
        lo, hi = RETURNS[g]
        swaps[g].wait()

        def one(i):
            o = pl.multiple_of((2 * i + s) * TOK, TOK)
            both[i] = (acc[pl.ds(o, TOK), :] + other[i].astype(f32)).astype(bf16)

            @pl.when(i == p)
            def _():
                pltpu.make_async_copy(both.at[i], kr.at[h, p % 2], sr).start()

            @pl.when(i != p)
            def _():
                block_copy(i).start()

        loop(lo, hi, one)

    def add(i):
        a, b = i // 4, i % 4
        hbuf[a, b] = (gm_ref[a, b, s].astype(f32) + rcm[a, b].astype(f32)).astype(bf16)

    chip.wait()
    loop(0, 16, add)
    sums = Reduce(hbuf, MLP_PARTS, r.mlp_bufs, r.ms, r.mr)
    sums.begin(0)
    for k in range(NQB):
        block(NQB - 1 - k)
        return_queries(NQB - 1 - k)
        exchange(k)
        if k > 0:
            push(k - 1)
        if k == 2:
            sums.end(0)
            sums.begin(1)
    push(NQB - 1)
    wait_for(both.at[pl.ds(0, 15)], ss)
    wait_for(cq, qs)
    wait_for(cq, qr)
    wait_for(kr, sr)
    sums.end(1)
    sums.begin(2)
    return sums


def momenta_starts():
    c = lax.axis_index("ctx")
    return jnp.minimum(48 * c // 128, 10), 16 * c // 128, 64 * c // 128


def momenta_loads(r):
    c = lax.axis_index("ctx")
    starts = momenta_starts()
    loads = []
    for k, (m, width) in enumerate(((r.mq, 256), (r.mo, 128), (r.mi, 128))):
        first = pl.multiple_of(starts[k] * 128, 128)
        loads.append(
            pltpu.make_async_copy(
                m.at[:, pl.ds(first, width)],
                r.mwin.at[:, pl.ds((0, 256, 384)[k], width)],
                r.msem.at[k],
            )
        )
    loads.append(pltpu.make_async_copy(r.mf.at[pl.ds(16 * c, 16)], r.mfin, r.msem.at[3]))
    return loads


def momenta_begin(r):
    for cp in momenta_loads(r):
        cp.start()


def momenta(r):
    c = lax.axis_index("ctx")
    for cp in momenta_loads(r):
        cp.wait()
    r.mtr[...] = r.mwin[...].T
    offset = 48 * c - momenta_starts()[0] * 128
    return jnp.concatenate(
        [
            r.mtr[pl.ds(pl.multiple_of(offset, 16), 48), :],
            r.mtr[pl.ds(pl.multiple_of(256 + 16 * c % 128, 16), 16), :],
            r.mtr[pl.ds(pl.multiple_of(384 + 64 * c % 128, 64), 64), :],
        ]
        + [r.mfin[:, 128 * b : 128 * b + 128] for b in range(4)],
        axis=0,
    )


def back_phase(r, mlp_sums):
    dqkv, gx, us, ur, v0, v1, vy, vz, vx = r.dqkv, r.gx, r.us, r.ur, r.v0, r.v1, r.vy, r.vz, r.vx
    cq_ref, kr_ref, w1, ga, rcm, hbuf = r.cq, r.kr, r.w1, r.gm, r.rcm, r.hbuf
    vs, vr, xs, xr, ua = r.vs, r.vr, r.us_s, r.us_r, r.w3
    att = pl.ds(0, 80)
    y, z, s, x = coords()
    c = lax.axis_index("ctx")
    xf, inv, normed, hidden = norm_parts(r.x, r.gain[...], r.shift[...])
    dy = r.dy[...]
    co, s1, s2 = r.co[...], -r.s1[...], -r.s2[...]
    left = lax.broadcasted_iota(jnp.int32, (TOK, 128), 1) < 64
    ctx = []
    for pair in range(4):
        a = cq_ref[2 * pair].astype(f32)
        b = cq_ref[2 * pair + 1].astype(f32)
        e = kr_ref[2 * pair, 0].astype(f32) + kr_ref[2 * pair, 1].astype(f32)
        f = kr_ref[2 * pair + 1, 0].astype(f32) + kr_ref[2 * pair + 1, 1].astype(f32)
        dq = jnp.where(left, a, pltpu.roll(b, 64, 1))
        dk = jnp.where(left, e, pltpu.roll(f, 64, 1))
        dqkv[:, 128 * pair : 128 * pair + 128] = turn(dq, co, s1, s2).astype(bf16)
        dqkv[:, 512 + 128 * pair : 640 + 128 * pair] = turn(dk, co, s1, s2).astype(bf16)
        dqkv[:, 1024 + 128 * pair : 1152 + 128 * pair] = jnp.where(
            left, pltpu.roll(e, 64, 1), f
        ).astype(bf16)
        ctx.append(jnp.where(left, pltpu.roll(a, 64, 1), b).astype(bf16))
    ctx = jnp.concatenate(ctx, axis=1)
    r.hid[...] = ctx
    hi, lo = split(dot_tn(dy, ctx))
    hi, lo = hi.reshape(4, 4, 2, 16, 512), lo.reshape(4, 4, 2, 16, 512)
    for b in range(4):
        lanes = slice(128 * b, 128 * b + 128)
        ga[:, :, :, b, 48:64] = hi[..., lanes]
        ga[:, :, :, b, 64:80] = lo[..., lanes]
    for i in range(4):
        part = dqkv[:, 384 * i : 384 * i + 384]
        g = dot_tn(part, hidden).astype(bf16).reshape(4, 2, 48, 512)
        for b in range(4):
            ga[i, :, :, b, 0:48] = g[..., 128 * b : 128 * b + 128]
    chip = send(ga.at[:, :, 1 - s, :, att], rcm.at[:, :, :, att], r.m_s.at[1], r.m_r.at[1], other_core())
    r.out[...] = (r.res[...] + dot(rolled(r.hid, x), wide(w1, 12, 4))).astype(bf16)
    dh = r.dh[...]
    for third in range(3):
        part = dqkv[:, 512 * third : 512 * third + 512]
        dh = dh + dot_nt(part, wide(w1, 4 * third, 4))
        v0[2 + third : 3 + third, :] = jnp.sum(part.astype(f32), axis=0, keepdims=True)
    dh = unroll(dh, r.wide_f, x)
    scaled = dh * r.gain[...]
    dyf = dy.astype(f32)
    r.gt[...] = dyf + inv * (
        scaled
        - jnp.mean(scaled, axis=1, keepdims=True)
        - normed * jnp.mean(scaled * normed, axis=1, keepdims=True)
    )
    dsum = jnp.sum(dyf, axis=0, keepdims=True)
    v0[0:1, :] = jnp.sum(dh * normed, axis=0, keepdims=True)
    v0[1:2, :] = jnp.sum(dh, axis=0, keepdims=True)
    v0[5:6, :] = dsum
    v0[10:11, :] = dsum
    v0[11:16, :] = jnp.zeros((5, 512), f32)
    chip.wait()
    vcp = [send(v0, v1, vs.at[0], vr.at[0], other_core())]

    def add(i):
        a, b = i // 4, i % 4
        both = ga[a, b, s, :, 0:80].astype(f32) + rcm[a, b, :, 0:80].astype(f32)
        hi, lo = split(both[:, 48:64] + both[:, 64:80])
        hbuf[a, b, :, 0:48] = both[:, 0:48].astype(bf16)
        hbuf[a, b, :, 48:64] = hi
        hbuf[a, b, :, 64:80] = lo

    loop(0, 16, add)
    sums = Reduce(hbuf, ATT_PARTS, r.att_bufs, r.as_, r.ar)
    sums.begin(0)
    mt = momenta(r)

    def vec_stage(k, buf, axis):
        for cp in vcp:
            cp.wait()
        vcp.clear()
        if k == 0:
            v = v0[...] + v1[...]
        else:
            last = (vy, vz)[k - 1]
            v = (last[0] + last[1]) + (last[2] + last[3])
        place = {"y": y, "z": z, "x": x}[axis]
        buf[place] = v
        for d in (1, 2, 3):
            vcp.append(
                send(buf.at[place], buf.at[place], vs.at[3 * k + d], vr.at[3 * k + d], moved(axis, d))
            )

    sums.end(0)
    sums.begin(1)
    vec_stage(0, vy, "y")
    sums.end(1)
    sums.begin(2)
    vec_stage(1, vz, "z")
    lo = 64
    for v in mlp_sums.end(2):
        gx[lo : lo + v.shape[0], :] = v
        lo += v.shape[0]
    g = sums.end(2)
    gx[0:32, :] = g[0]
    gx[32:48, :] = g[1]
    gx[48:64, :] = g[2]
    grad = gx[...]
    u = (1.0 + MU) * grad + (MU * MU) * mt
    ub = u.astype(bf16)
    hi, lo = split(u[48:64])
    us[0, 0:48] = ub[0:48]
    us[0, 48:64] = jnp.zeros((16, 128), bf16)
    us[1, 0:16] = hi
    us[1, 16:32] = lo
    us[1, 32:64] = jnp.zeros((32, 128), bf16)
    us[2] = ub[64:128]
    us[3] = ub[128:192]
    cps = []
    for d in (1, 2, 3):
        cps.append(send(us.at[(x + d) % 4], ur.at[x], xs.at[d - 1], xr.at[d - 1], moved("x", d)))
    vec_stage(2, vx, "x")
    ur[x] = us[x]
    r.gxa[y, z, s] = grad.astype(bf16)
    for cp in cps:
        cp.wait()
    for k in range(4):
        piece = ur[k]

        @pl.when(x != 3)
        def _(k=k, piece=piece):
            ua[:, y, z, s, :, 128 * k : 128 * k + 128] = piece.reshape(4, 16, 128)

        @pl.when(x == 3)
        def _(k=k, piece=piece):
            for b in range(4):
                ua[k, y, z, s, :, 128 * b : 128 * b + 128] = piece[16 * b : 16 * b + 16]

    gather = Gather(
        [
            (lambda a, b, e: ua.at[pl.ds(0, 2), a, b, e], True),
            (lambda a, b, e: ua.at[pl.ds(2, 2), a, b, e], False),
        ],
        r.sa, r.ra,
    )
    gather.begin()
    for cp in vcp:
        cp.wait()
    r.vec[...] = (vx[0] + vx[1]) + (vx[2] + vx[3])
    gather.turn()
    gather.pass_on()
    gather.end()


def dot3(a, b):
    (ah, al), (bh, bl) = a, b
    return dot(ah, bh) + (dot(ah, bl) + dot(al, bh))


def newton_phase(r):
    y, z, s, x = coords()
    ua, ga, oa, a_ref = r.w3, r.gxa, r.oa, r.a
    ah, al, ph, pl_, th, tl, uh, ul = r.ah, r.al, r.ph, r.pl, r.th, r.tl, r.uh, r.ul
    os, rows, xs, xr = r.os, r.rows, r.os_s, r.os_r
    grads = Gather(
        [
            (lambda a, b, e: ga.at[a, b, e, pl.ds(0, 96)], True),
            (lambda a, b, e: ga.at[a, b, e, pl.ds(96, 96)], False),
        ],
        r.sb, r.rb,
    )
    grads.begin()

    def load(hi, lo):
        return hi[...], lo[...]

    def store(hi, lo, v):
        h, l = split(v)
        hi[...] = h
        lo[...] = l

    @pl.when(x == 1)
    def _():
        uh[...] = ua[0].reshape(512, 512)
        ul[...] = ua[1].reshape(512, 512)
        h, l = uh[...], ul[...]
        a_ref[...] = dot_tn(h, h) + (dot_tn(h, l) + dot_tn(l, h))

    @pl.when(x != 1)
    def _():
        u = ua[...].reshape(2048, 512)
        a_ref[...] = dot_tn(u, u)

    row = lax.broadcasted_iota(jnp.int32, (512, 512), 0)
    col = lax.broadcasted_iota(jnp.int32, (512, 512), 1)
    eye = row == col
    a = a_ref[...]
    square = jnp.sum(jnp.sum(jnp.where(eye, a, 0.0), axis=0, keepdims=True), axis=1, keepdims=True)
    scale = 1.0 / (jnp.sqrt(square) + 1e-07)
    a_ref[...] = a * (scale * scale)
    mine = ua[:, y, z, s].reshape(64, 512).astype(f32) * scale

    def poly():
        store(ah, al, a_ref[...])
        sq = dot3(load(ah, al), load(ah, al))
        return C2 * a_ref[...] + C3 * sq + jnp.where(eye, C1, 0.0)

    def step(_, mine):
        store(ph, pl_, poly())
        pair = load(ph, pl_)
        store(th, tl, dot3(pair, load(ah, al)))
        a_ref[...] = dot3(pair, load(th, tl))
        return dot3(split(mine), pair)

    mine = lax.fori_loop(0, 2, step, mine)
    grads.turn()
    mine = lax.fori_loop(2, NS_ITERS - 1, step, mine)
    grads.pass_on()
    store(ph, pl_, poly())
    mine = dot3(split(mine), load(ph, pl_))
    side = jnp.where(x == 0, math.sqrt(1536.0), jnp.where(x == 1, math.sqrt(512.0), math.sqrt(2048.0)))
    mine = mine * (0.2 * side)
    mine = jnp.concatenate(
        [jnp.where(x == 1, mine[0:16] + mine[16:32], mine[0:16]), mine[16:64]], axis=0
    ).astype(bf16)
    for k in range(4):
        by_lanes = mine[:, 128 * k : 128 * k + 128]
        by_rows = jnp.concatenate(
            [mine[16 * k : 16 * k + 16, 128 * b : 128 * b + 128] for b in range(4)], axis=0
        )
        os[k] = jnp.where(x == 3, by_rows, by_lanes)
    cps = []
    for d in (1, 2, 3):
        cps.append(send(os.at[(x + d) % 4], rows.at[x], xs.at[d - 1], xr.at[d - 1], moved("x", d)))
    rows[x] = os[x]
    grads.end()
    for cp in cps:
        cp.wait()
    oa[y, z, s, 0:48] = rows[0, 0:48]
    oa[y, z, s, 48:64] = rows[1, 0:16]
    oa[y, z, s, 64:128] = rows[2]
    oa[y, z, s, 128:192] = rows[3]
    update = Gather(
        [
            (lambda a, b, e: oa.at[a, b, e, pl.ds(0, 96)], True),
            (lambda a, b, e: oa.at[a, b, e, pl.ds(96, 96)], False),
        ],
        r.se, r.re,
    )
    update.begin()
    update.turn()
    update.pass_on()
    update.end()


def scratch_list():
    V = pltpu.VMEM
    piece = (HEADS, TOK, 128)
    out = [
        ("fq", V((128, 1536), f32)), ("fo", V((128, 512), f32)),
        ("fi", V((128, 2048), f32)), ("ff", V((512, 512), f32)),
        ("x", V((TOK, D), bf16)), ("dy", V((TOK, D), bf16)),
        ("w1", V((4, 4, 4, 2, 64, 128), bf16)), ("w2", V((4, 4, 4, 2, 64, 128), bf16)),
        ("w3", V((4, 4, 4, 2, 16, 512), bf16)),
        ("kvs", V(piece, bf16)), ("qds", V(piece, bf16)),
        ("kv", V((GROUP, 128), bf16)), ("qd", V((NQB, QB, 128), bf16)),
        ("hid", V((TOK, D), bf16)), ("wide_f", V((TOK, D), f32)),
        ("co", V((TOK, 128), f32)), ("s1", V((TOK, 128), f32)), ("s2", V((TOK, 128), f32)),
        ("res", V((TOK, D), f32)), ("dh", V((TOK, D), f32)),
        ("gm", V((4, 4, 2, 4, 128, 128), bf16)),
        ("rcm", V((4, 4, 4, 128, 128), bf16)), ("hbuf", V((4, 4, 4, 128, 128), bf16)),
        ("kvt", V((128, GROUP), bf16)), ("acc", V((GROUP, 128), f32)),
        ("s_sc", V((GROUP, QB), f32)), ("p_sc", V((GROUP, QB), f32)),
        ("m_sc", V((GROUP // HB, 8, QB), f32)), ("cqs", V((NQB, QB, 128), bf16)),
        ("half", V((16, TOK, 128), bf16)), ("other", V((16, TOK, 128), bf16)),
        ("both", V((16, TOK, 128), bf16)),
        ("spare", V((6, 64, 128), bf16)),
        ("cq", V(piece, bf16)), ("kr", V((HEADS, 2, TOK, 128), bf16)),
        ("dqkv", V((TOK, 1536), bf16)),
        ("mwin", V((128, 512), f32)), ("mtr", V((512, 128), f32)), ("mfin", V((16, 512), f32)),
        ("gx", V((192, 128), f32)),
        ("us", V((4, 64, 128), bf16)), ("ur", V((4, 64, 128), bf16)),
        ("os", V((4, 64, 128), bf16)), ("rows", V((4, 64, 128), bf16)),
        ("v0", V((16, 512), f32)), ("v1", V((16, 512), f32)),
        ("vy", V((4, 16, 512), f32)), ("vz", V((4, 16, 512), f32)), ("vx", V((4, 16, 512), f32)),
        ("a", V((512, 512), f32)),
    ]
    out += [(k, V((512, 512), bf16)) for k in ("ah", "al", "ph", "pl", "th", "tl", "uh", "ul")]
    for name, shape in (
        ("lsem", (6,)), ("msem", (4,)), ("xs", (5, 3)), ("xr", (5, 3)), ("ys", (3, 3)), ("yr", (3, 3)),
        ("sa", (2, 3)), ("ra", (2, 5)), ("sb", (2, 3)), ("rb", (2, 5)),
        ("se", (2, 3)), ("re", (2, 5)),
        ("own_sem", None), ("ks", None), ("kvr", None), ("qs", None), ("qr", None),
        ("cs", None), ("cr", None),
        ("m_s", (2,)), ("m_r", (2,)), ("ms", (3, 3)), ("mr", (3, 3)), ("as_", (3, 3)), ("ar", (3, 3)),
        ("ws", (6,)), ("wr", (6,)), ("bs", None), ("br", None), ("rqs", None), ("rqr", None),
        ("vs", (10,)), ("vr", (10,)), ("us_s", (3,)), ("us_r", (3,)), ("os_s", (3,)), ("os_r", (3,)),
    ):
        out.append((name, DMA if shape is None else DMA(shape)))
    out += [(f"mlp{i}", v) for i, v in enumerate(Reduce.scratch(MLP_PARTS))]
    out += [(f"att{i}", v) for i, v in enumerate(Reduce.scratch(ATT_PARTS))]
    return out


INPUTS = (
    "starts", "x_in", "dy_in", "gain", "shift", "bias", "wq", "wo", "wi", "wf", "mq", "mo", "mi", "mf",
)
OUTPUTS = ("out", "gt", "gxa", "oa", "vec")


def step_kernel(names, *refs):
    r = types.SimpleNamespace(**dict(zip(names, refs)))
    r.mlp_bufs = [getattr(r, f"mlp{i}") for i in range(5 * len(MLP_PARTS))]
    r.att_bufs = [getattr(r, f"att{i}") for i in range(5 * len(ATT_PARTS))]
    chip = front_phase(r)
    back_phase(r, attention_phase(r, chip))
    newton_phase(r)


def train_step(*args):
    scratch = scratch_list()
    names = INPUTS + OUTPUTS + tuple(k for k, _ in scratch)
    return pl.pallas_call(
        functools.partial(step_kernel, names),
        out_shape=tuple(
            jax.ShapeDtypeStruct(shape, t)
            for shape, t in (
                ((TOK, D), bf16), ((TOK, D), f32),
                ((4, 4, 2, 192, 128), bf16), ((4, 4, 2, 192, 128), bf16), ((16, 512), f32),
            )
        ),
        in_specs=[SM, ANY, ANY, VM, VM, VM] + [ANY] * 8,
        out_specs=(VM,) * 5,
        scratch_shapes=[v for _, v in scratch],
        compiler_params=pltpu.CompilerParams(
            vmem_limit_bytes=63 * 2**20, collective_id=1, has_side_effects=True
        ),
        name="train_step",
    )(*args)


def update_kernel(
    gx, oa, out, gt, wq, wo, wi, wf, mq, mo, mi, mf, vec, vm, gain, shift, bias,
    out_to, gt_to, nmq, nwq, nmo, nwo, nmi, nwi, nmf, nwf, nvm, nvec,
):
    out_to[...] = out[...]
    gt_to[...] = gt[...]

    @pl.when(pl.program_id(0) == 0)
    def _():
        for k in range(11):
            part = slice(512 * k, 512 * k + 512)
            v = VMU * vm[part] + vec[k]
            old = (gain[...], shift[...])[k] if k < 2 else bias[512 * k - 1024 : 512 * k - 512]
            nvm[part] = v
            nvec[part] = old - VLR * v

    for lo, n, w, m, nm, nw in (
        (0, 48, wq, mq, nmq, nwq),
        (48, 16, wo, mo, nmo, nwo),
        (64, 64, wi, mi, nmi, nwi),
    ):
        grad = gx[:, lo : lo + n, :].astype(f32).reshape(8 * n, 128).T
        turned = oa[:, lo : lo + n, :].astype(f32).reshape(8 * n, 128).T
        nm[...] = MU * m[...] + grad
        nw[...] = (1.0 - LR * WD) * w[...] - LR * turned
    for b in range(4):
        cols = slice(128 * b, 128 * b + 128)
        rows = slice(128 + 16 * b, 144 + 16 * b)
        grad = gx[:, rows, :].astype(f32).reshape(128, 128)
        turned = oa[:, rows, :].astype(f32).reshape(128, 128)
        nmf[:, cols] = MU * mf[:, cols] + grad
        nwf[:, cols] = (1.0 - LR * WD) * wf[:, cols] - LR * turned


def update(gx, oa, out, gt, weights, moments, vec, vec_mom, gain, shift, biases):
    def whole(v):
        return pl.BlockSpec(v.shape, lambda i, n=v.ndim: (0,) * n)

    piece = pl.BlockSpec((8, 192, 128), lambda i: (i, 0, 0))
    rows = pl.BlockSpec((48, D), lambda i: (i, 0))
    blocks = [
        pl.BlockSpec((128, 384), lambda i: (0, i)),
        pl.BlockSpec((128, 128), lambda i: (0, i)),
        pl.BlockSpec((128, 512), lambda i: (0, i)),
        pl.BlockSpec((128, 512), lambda i: (i, 0)),
    ]
    shape = lambda v: jax.ShapeDtypeStruct(v.shape, v.dtype)
    outs, specs = [shape(out), shape(gt)], [rows, rows]
    for w, b in zip(weights, blocks):
        outs += [shape(w)] * 2
        specs += [b, b]
    outs += [shape(vec_mom)] * 2
    specs += [whole(vec_mom)] * 2
    vectors = (vec, vec_mom, gain, shift, biases)
    return pl.pallas_call(
        update_kernel,
        grid=(4,),
        out_shape=tuple(outs),
        in_specs=[piece, piece, rows, rows] + blocks + blocks + [whole(v) for v in vectors],
        out_specs=tuple(specs),
        compiler_params=pltpu.CompilerParams(vmem_limit_bytes=60 * 2**20),
        name="update_weights",
    )(gx, oa, out, gt, *weights, *moments, *vectors)


def body(
    tokens, cotangent, ln_gain, ln_bias, biases, w_qkv, w_out, w_in, w_fin,
    mom_qkv, mom_out, mom_in, mom_fin, vec_mom, starts,
):
    weights = (w_qkv, w_out, w_in, w_fin)
    moments = (mom_qkv, mom_out, mom_in, mom_fin)
    block_out, grad_tokens, gx, oa, vec_sum = train_step(
        starts, tokens, cotangent, ln_gain[None, :], ln_bias[None, :], biases, *weights, *moments
    )
    return update(
        gx.reshape(32, 192, 128), oa.reshape(32, 192, 128), block_out, grad_tokens,
        weights, moments, vec_sum, vec_mom, ln_gain, ln_bias, biases,
    )


def solution(mesh):
    tok = P(("wsh", "ctx"), None)
    row = P("wsh", None)
    return jax.shard_map(
        body,
        mesh=mesh,
        in_specs=(tok, tok, P(), P(), P()) + (row,) * 8 + (P(), P()),
        out_specs=(tok, tok) + (row,) * 8 + (P(), P()),
        check_vma=False,
    )
```

profile of v0, /device:TPU:1, one launch (start us, length us, event | category | flops | bytes accessed | tf_op | source)
XLA Modules:
  0.0 171.0 jit_solution(16738876051255503312)
XLA Ops:
  0.6 163.1 %train_step.1 = (bf16[192,512]{1,0:T(8,128)(2,1)}, f32[192,512]{1,0:T(8,128)}, bf16[4,4,2,192,128]{4,3,2,1,0:T(8,128)(2,1)}, bf16[4,4,2,192,128]{4,3,2,1,0:T(8,128)(2,1)}, f32[16,512]{1,0:T(8,128)}) custom-call(s32[4]{0:T(128)} %refs_0_.1, bf16[192,512]{1,0:T(8,128)(2,1)} %refs_1_.1, bf16[192,512]{1,0:T(8,128)(2,1)} %refs_2_.1, f32[1,512]{1,0:T(1,128)} %bitcast.6, ...), custom_call_target="tpu_custom_call" | custom-call | tf_op jit(solution)/shard_map/train_step/pallas_call | solution.py:1043
  163.7 7.1 %update_weights.1 = (bf16[192,512]{1,0:T(8,128)(2,1)}, f32[192,512]{1,0:T(8,128)}, f32[128,1536]{1,0:T(8,128)}, f32[128,1536]{1,0:T(8,128)}, f32[128,512]{1,0:T(...) custom-call(bf16[32,192,128]{2,1,0:T(8,128)(2,1)} %bitcast.4, ...), custom_call_target="tpu_custom_call" | custom-call | tf_op jit(solution)/shard_map/update_weights/pallas_call | solution.py:1116
where the time goes:
time: 171 us
  Pallas kernels  170 us (99%)
    pallas_call x1, Pallas kernels, train_step(): pl.pallas_call(functools.partial(step_kernel, names), out_shape=tuple((ja...  163 us
    pallas_call x1, Pallas kernels, update(): pl.pallas_call(update_kernel, grid=(4,), out_shape=tuple(outs), in_specs=...  7.13 us

commit v1 on v0

--- a/solution.py
+++ b/solution.py
@@ -653,17 +653,18 @@
         a, b = i // 4, i % 4
         hbuf[a, b] = (gm_ref[a, b, s].astype(f32) + rcm[a, b].astype(f32)).astype(bf16)
 
-    chip.wait()
-    loop(0, 16, add)
     sums = Reduce(hbuf, MLP_PARTS, r.mlp_bufs, r.ms, r.mr)
-    sums.begin(0)
     for k in range(NQB):
         block(NQB - 1 - k)
         return_queries(NQB - 1 - k)
         exchange(k)
         if k > 0:
             push(k - 1)
-        if k == 2:
+        if k == 0:
+            chip.wait()
+            loop(0, 16, add)
+            sums.begin(0)
+        if k == 3:
             sums.end(0)
             sums.begin(1)
     push(NQB - 1)
@@ -718,6 +719,11 @@
         + [r.mfin[:, 128 * b : 128 * b + 128] for b in range(4)],
         axis=0,
     )
+
+
+def leave(r, k):
+    src, dst = ((r.out, r.out_to), (r.gt, r.gt_to), (r.gxa, r.gxa_to))[k]
+    return pltpu.make_async_copy(src, dst, r.osem.at[k])
 
 
 def back_phase(r, mlp_sums):
@@ -773,6 +779,8 @@
         - jnp.mean(scaled, axis=1, keepdims=True)
         - normed * jnp.mean(scaled * normed, axis=1, keepdims=True)
     )
+    leave(r, 0).start()
+    leave(r, 1).start()
     dsum = jnp.sum(dyf, axis=0, keepdims=True)
     v0[0:1, :] = jnp.sum(dh * normed, axis=0, keepdims=True)
     v0[1:2, :] = jnp.sum(dh, axis=0, keepdims=True)
@@ -954,6 +962,7 @@
         cps.append(send(os.at[(x + d) % 4], rows.at[x], xs.at[d - 1], xr.at[d - 1], moved("x", d)))
     rows[x] = os[x]
     grads.end()
+    leave(r, 2).start()
     for cp in cps:
         cp.wait()
     oa[y, z, s, 0:48] = rows[0, 0:48]
@@ -971,6 +980,8 @@
     update.turn()
     update.pass_on()
     update.end()
+    for k in range(3):
+        leave(r, k).wait()
 
 
 def scratch_list():
@@ -1004,10 +1015,12 @@
         ("v0", V((16, 512), f32)), ("v1", V((16, 512), f32)),
         ("vy", V((4, 16, 512), f32)), ("vz", V((4, 16, 512), f32)), ("vx", V((4, 16, 512), f32)),
         ("a", V((512, 512), f32)),
+        ("out", V((TOK, D), bf16)), ("gt", V((TOK, D), f32)),
+        ("gxa", V((4, 4, 2, 192, 128), bf16)),
     ]
     out += [(k, V((512, 512), bf16)) for k in ("ah", "al", "ph", "pl", "th", "tl", "uh", "ul")]
     for name, shape in (
-        ("lsem", (6,)), ("msem", (4,)), ("xs", (5, 3)), ("xr", (5, 3)), ("ys", (3, 3)), ("yr", (3, 3)),
+        ("lsem", (6,)), ("osem", (3,)), ("msem", (4,)), ("xs", (5, 3)), ("xr", (5, 3)), ("ys", (3, 3)), ("yr", (3, 3)),
         ("sa", (2, 3)), ("ra", (2, 5)), ("sb", (2, 3)), ("rb", (2, 5)),
         ("se", (2, 3)), ("re", (2, 5)),
         ("own_sem", None), ("ks", None), ("kvr", None), ("qs", None), ("qr", None),
@@ -1025,7 +1038,7 @@
 INPUTS = (
     "starts", "x_in", "dy_in", "gain", "shift", "bias", "wq", "wo", "wi", "wf", "mq", "mo", "mi", "mf",
 )
-OUTPUTS = ("out", "gt", "gxa", "oa", "vec")
+OUTPUTS = ("out_to", "gt_to", "gxa_to", "oa", "vec")
 
 
 def step_kernel(names, *refs):
@@ -1050,7 +1063,7 @@
             )
         ),
         in_specs=[SM, ANY, ANY, VM, VM, VM] + [ANY] * 8,
-        out_specs=(VM,) * 5,
+        out_specs=(ANY, ANY, ANY, VM, VM),
         scratch_shapes=[v for _, v in scratch],
         compiler_params=pltpu.CompilerParams(
             vmem_limit_bytes=63 * 2**20, collective_id=1, has_side_effects=True

time: 171 us -> 171 us (level)
  no operation moved by 1% of the time
where the time goes in v1:
time: 171 us; the launch traced here: 170 us
  Pallas kernels  170 us (99%)
    pallas_call x1, Pallas kernels, train_step(): pl.pallas_call(functools.partial(step_kernel, names), out_shape=tuple((ja...  162 us
    pallas_call x1, Pallas kernels, update(): pl.pallas_call(update_kernel, grid=(4,), out_shape=tuple(outs), in_specs=...  7.13 us

profile of v1, /device:TPU:1, one launch (start us, length us, event | category | flops | bytes accessed | tf_op | source)
XLA Modules:
  0.0 170.4 jit_solution(16819747382732485739)
XLA Ops:
  0.6 162.4 %train_step.1 = (bf16[192,512]{1,0:T(8,128)(2,1)}, f32[192,512]{1,0:T(8,128)}, bf16[4,4,2,192,128]{4,3,2,1,0:T(8,128)(2,1)}, bf16[4,4,2,192,128]{4,3,2,1,0:T(8,128)(2,1)}, f32[16,512]{1,0:T(8,128)}) custom-call(s32[4]{0:T(128)} %refs_0_.1, bf16[192,512]{1,0:T(8,128)(2,1)} %refs_1_.1, bf16[192,512]{1,0:T(8,128)(2,1)} %refs_2_.1, f32[1,512]{1,0:T(1,128)} %bitcast.6, ...), custom_call_target="tpu_custom_call" | custom-call | tf_op jit(solution)/shard_map/train_step/pallas_call | solution.py:1056
  163.0 7.1 %update_weights.1 = (bf16[192,512]{1,0:T(8,128)(2,1)}, f32[192,512]{1,0:T(8,128)}, f32[128,1536]{1,0:T(8,128)}, f32[128,1536]{1,0:T(8,128)}, f32[128,512]{1,0:T(...) custom-call(bf16[32,192,128]{2,1,0:T(8,128)(2,1)} %bitcast.4, ...), custom_call_target="tpu_custom_call" | custom-call | tf_op jit(solution)/shard_map/update_weights/pallas_call | solution.py:1129

commit v2 on v1

--- a/solution.py
+++ b/solution.py
@@ -668,8 +668,6 @@
             sums.end(0)
             sums.begin(1)
     push(NQB - 1)
-    wait_for(both.at[pl.ds(0, 15)], ss)
-    wait_for(cq, qs)
     wait_for(cq, qr)
     wait_for(kr, sr)
     sums.end(1)
@@ -877,7 +875,9 @@
     r.vec[...] = (vx[0] + vx[1]) + (vx[2] + vx[3])
     gather.turn()
     gather.pass_on()
+    gram(r, s, False)
     gather.end()
+    gram(r, 1 - s, True)
 
 
 def dot3(a, b):
@@ -885,10 +885,27 @@
     return dot(ah, bh) + (dot(ah, bl) + dot(al, bh))
 
 
+def gram(r, e, more):
+    x = lax.axis_index("wsh")
+
+    def put(v):
+        r.a[...] = r.a[...] + v if more else v
+
+    @pl.when(x == 1)
+    def _():
+        h, l = r.w3[0, :, :, e].reshape(256, 512), r.w3[1, :, :, e].reshape(256, 512)
+        put(dot_tn(h, h) + (dot_tn(h, l) + dot_tn(l, h)))
+
+    @pl.when(x != 1)
+    def _():
+        u = r.w3[:, :, :, e].reshape(1024, 512)
+        put(dot_tn(u, u))
+
+
 def newton_phase(r):
     y, z, s, x = coords()
     ua, ga, oa, a_ref = r.w3, r.gxa, r.oa, r.a
-    ah, al, ph, pl_, th, tl, uh, ul = r.ah, r.al, r.ph, r.pl, r.th, r.tl, r.uh, r.ul
+    ah, al, ph, pl_, th, tl = r.ah, r.al, r.ph, r.pl, r.th, r.tl
     os, rows, xs, xr = r.os, r.rows, r.os_s, r.os_r
     grads = Gather(
         [
@@ -906,18 +923,6 @@
         h, l = split(v)
         hi[...] = h
         lo[...] = l
-
-    @pl.when(x == 1)
-    def _():
-        uh[...] = ua[0].reshape(512, 512)
-        ul[...] = ua[1].reshape(512, 512)
-        h, l = uh[...], ul[...]
-        a_ref[...] = dot_tn(h, h) + (dot_tn(h, l) + dot_tn(l, h))
-
-    @pl.when(x != 1)
-    def _():
-        u = ua[...].reshape(2048, 512)
-        a_ref[...] = dot_tn(u, u)
 
     row = lax.broadcasted_iota(jnp.int32, (512, 512), 0)
     col = lax.broadcasted_iota(jnp.int32, (512, 512), 1)
@@ -1018,7 +1023,7 @@
         ("out", V((TOK, D), bf16)), ("gt", V((TOK, D), f32)),
         ("gxa", V((4, 4, 2, 192, 128), bf16)),
     ]
-    out += [(k, V((512, 512), bf16)) for k in ("ah", "al", "ph", "pl", "th", "tl", "uh", "ul")]
+    out += [(k, V((512, 512), bf16)) for k in ("ah", "al", "ph", "pl", "th", "tl")]
     for name, shape in (
         ("lsem", (6,)), ("osem", (3,)), ("msem", (4,)), ("xs", (5, 3)), ("xr", (5, 3)), ("ys", (3, 3)), ("yr", (3, 3)),
         ("sa", (2, 3)), ("ra", (2, 5)), ("sb", (2, 3)), ("rb", (2, 5)),
@@ -1047,6 +1052,8 @@
     r.att_bufs = [getattr(r, f"att{i}") for i in range(5 * len(ATT_PARTS))]
     chip = front_phase(r)
     back_phase(r, attention_phase(r, chip))
+    wait_for(r.both.at[pl.ds(0, 15)], r.bs)
+    wait_for(r.cq, r.rqs)
     newton_phase(r)
 
 

time: 171 us -> 170 us (level)
  no operation moved by 1% of the time
where the time goes in v2:
time: 170 us
  Pallas kernels  169 us (99%)
    pallas_call x1, Pallas kernels, train_step(): pl.pallas_call(functools.partial(step_kernel, names), out_shape=tuple((ja...  162 us
    pallas_call x1, Pallas kernels, update(): pl.pallas_call(update_kernel, grid=(4,), out_shape=tuple(outs), in_specs=...  7.13 us

profile of v2, /device:TPU:1, one launch (start us, length us, event | category | flops | bytes accessed | tf_op | source)
XLA Modules:
  0.0 169.8 jit_solution(4516282069566404903)
XLA Ops:
  0.6 161.8 %train_step.1 = (bf16[192,512]{1,0:T(8,128)(2,1)}, f32[192,512]{1,0:T(8,128)}, bf16[4,4,2,192,128]{4,3,2,1,0:T(8,128)(2,1)}, bf16[4,4,2,192,128]{4,3,2,1,0:T(8,128)(2,1)}, f32[16,512]{1,0:T(8,128)}) custom-call(s32[4]{0:T(128)} %refs_0_.1, bf16[192,512]{1,0:T(8,128)(2,1)} %refs_1_.1, bf16[192,512]{1,0:T(8,128)(2,1)} %refs_2_.1, f32[1,512]{1,0:T(1,128)} %bitcast.6, ...), custom_call_target="tpu_custom_call" | custom-call | tf_op jit(solution)/shard_map/train_step/pallas_call | solution.py:1063
  162.5 7.1 %update_weights.1 = (bf16[192,512]{1,0:T(8,128)(2,1)}, f32[192,512]{1,0:T(8,128)}, f32[128,1536]{1,0:T(8,128)}, f32[128,1536]{1,0:T(8,128)}, f32[128,512]{1,0:T(...) custom-call(bf16[32,192,128]{2,1,0:T(8,128)(2,1)} %bitcast.4, ...), custom_call_target="tpu_custom_call" | custom-call | tf_op jit(solution)/shard_map/update_weights/pallas_call | solution.py:1136
